TPU v7x, 512 devices: a whole 4x4x16 slice. The times are simulated.
512 devices in a mesh: row: 32 (over z, core), col: 16 (over x, y).
Axes of the slice: x: 4, y: 4, z: 16, core: 2. Of those that a mesh axis runs over, the one named last changes fastest.
Arguments:
- matrix: float32 [8192, 8192], P('row', 'col'), may hold values from -6 to 6
- pivots: int32 [3, 256], replicated, may hold values from 0 to 8191, as said below
- inverses: float32 [3, 256, 256], replicated, may hold values from -0.0234375 to 0.0234375
Outputs:
- factored: float32 [8192, 8192], P('row', 'col')
Inputs may be any that keep to these rules, and one draw needn't show every extreme that they name: For panel k and position i, pivots[k, i] is either k * 256 + i or a row of index (k + 1) * 256 or more; position 0 of every panel is k * 256; no row is named twice within one panel; every panel names row 8191.
All inputs are finite; a program needn't handle non-finite values.
Results may differ from a plain program's by a relative error of at most 0.00017.
Values sent between devices are 32-bit elements; how exact they have to be, the bound alone decides.
A program may use at most 64 MiB of HBM per device.

v0:
```python
import jax
import jax.numpy as jnp
from jax import lax
from jax.sharding import PartitionSpec as P


def broadcast(array, axis, root):
    mine = lax.axis_index(axis) == root
    return lax.psum(jnp.where(mine, array, jnp.zeros_like(array)), axis)


def on_device(matrix, pivots, inverses):
    rows_here, cols_here = matrix.shape
    block = inverses.shape[1]
    nrow = lax.axis_size("row")
    ncol = lax.axis_size("col")
    rank_row = lax.axis_index("row")
    rank_col = lax.axis_index("col")
    local_rows = jnp.arange(rows_here, dtype=jnp.int32)
    global_rows = (local_rows // block * nrow + rank_row) * block + local_rows % block
    col_index = jnp.arange(cols_here, dtype=jnp.int32)
    global_cblock = col_index // block * ncol + rank_col
    offsets = jnp.arange(block, dtype=jnp.int32)
    current = matrix
    for panel in range(pivots.shape[0]):
        top = panel * block
        chosen = pivots[panel]
        stay = chosen == top + offsets
        owner = chosen // block % nrow
        local_pick = chosen // block // nrow * block + chosen % block
        local_pick = jnp.clip(local_pick, 0, rows_here - 1)
        picked = jnp.where((owner == rank_row)[:, None], current[local_pick], 0.0)
        diag_owner = panel % nrow
        diag_local = panel // nrow * block
        diag_block = current
        upper = lax.psum(picked, "row")
        displaced = broadcast(diag_block, "row", diag_owner)
        matches = (global_rows[:, None] == chosen[None, :]) & jnp.logical_not(stay)[None, :]
        has_match = jnp.any(matches, axis=1)
        source = jnp.sum(jnp.where(matches, offsets[None, :], 0), axis=1)
        in_diag = (global_rows >= top) & (global_rows < top + block)
        diag_pos = jnp.clip(global_rows - top, 0, block - 1)
        swapped = jnp.where(
            has_match[:, None],
            displaced[source],
            jnp.where(in_diag[:, None], upper[diag_pos], current),
        )
        col_owner = panel % ncol
        col_local = panel // ncol * block
        strip = swapped[:, col_local : col_local + block]
        below = (global_rows >= top + block)[:, None]
        made = jnp.where(
            below,
            jnp.dot(
                strip,
                inverses[panel],
                precision=lax.Precision.HIGHEST,
                preferred_element_type=jnp.float32,
            ),
            0.0,
        )
        factor = broadcast(made, "col", col_owner)
        replaced = jnp.where(below & (rank_col == col_owner), factor, strip)
        swapped = swapped.at[:, col_local : col_local + block].set(replaced)
        update = jnp.dot(
            factor, upper, precision=lax.Precision.HIGHEST, preferred_element_type=jnp.float32
        )
        current = swapped - jnp.where((global_cblock > panel)[None, :], update, 0.0)
    return current


def solution(mesh):
    placed = (P("row", "col"), P(), P())
    return jax.shard_map(
        on_device, mesh=mesh, in_specs=placed, out_specs=P("row", "col"), check_vma=False
    )
```

profile of v0, /device:TPU:2, one launch (start us, length us, event | category | flops | bytes accessed | tf_op | source)
XLA Modules:
  0.0 1026.0 jit_solution(13716612972238767918)
XLA Ops:
  6.5 0.8 fusion.45
  7.4 0.3 select_reduce_fusion
  7.7 0.1 compare_select_fusion.1
  7.8 1.9 broadcast_select_fusion.5
  9.8 1.0 gather_fusion.1
  10.7 0.9 broadcast_select_fusion.4
  11.7 0.0 all-reduce.20.cloned.1.call-update
  11.7 0.0 all-reduce.10.cloned.1.call-start
  11.8 0.3 fusion.17
  12.1 213.8 %all-reduce.20.cloned.1.call-done = (f32[256,512]{1,0:T(8,128)}, f32[256,512]{1,0:T(8,128)}) async-done(((f32[256,512]{1,0:T(8,128)}, f32[256,512]{1,0:T(8,128)}), (f32[256,512]{1,0:T(8,128)}, f32[256,512]{1,0:T(8,128)})) %all-reduce.20.cloned.1.call-update) | async-done | bytes 1048592 | tf_op jit(solution)/shard_map/psum | solution.py:9
  225.9 2.3 gather_fusion
  228.2 1.0 gather_fusion.2
  229.2 0.1 select_select_fusion.2
  229.4 1.0 copy-done.7
  230.3 1.1 fusion.5
  231.4 0.0 all-reduce.10.cloned.1.call-update
  231.5 0.0 all-reduce.18.cloned.1.call-start
  231.5 0.7 compare_reduce_fusion
  232.2 114.0 %all-reduce.10.cloned.1.call-done = f32[256,256]{1,0:T(8,128)} async-done(((f32[256,256]{1,0:T(8,128)}), f32[256,256]{1,0:T(8,128)}) %all-reduce.10.cloned.1.call-update) | async-done | bytes 262160 | tf_op jit(solution)/shard_map/psum | solution.py:9
  346.2 1.7 fusion.6
  347.9 1.5 broadcast_select_fusion.3
  349.4 1.0 gather_fusion.4
  350.4 0.9 broadcast_select_fusion.2
  351.3 0.0 all-reduce.18.cloned.1.call-update
  351.3 0.0 all-reduce.12.cloned.1.call-start
  351.5 210.3 %all-reduce.18.cloned.1.call-done = (f32[256,512]{1,0:T(8,128)}, f32[256,512]{1,0:T(8,128)}) async-done(((f32[256,512]{1,0:T(8,128)}, f32[256,512]{1,0:T(8,128)}), (f32[256,512]{1,0:T(8,128)}, f32[256,512]{1,0:T(8,128)})) %all-reduce.18.cloned.1.call-update) | async-done | bytes 1048592 | tf_op jit(solution)/shard_map/psum | solution.py:9
  561.8 2.3 gather_fusion.3
  564.1 1.0 gather_fusion.5
  565.1 0.1 select_select_fusion.1
  565.2 1.1 fusion.4
  566.3 0.0 all-reduce.12.cloned.1.call-update
  566.4 0.0 all-reduce.16.cloned.1.call-start
  566.4 114.7 %all-reduce.12.cloned.1.call-done = f32[256,256]{1,0:T(8,128)} async-done(((f32[256,256]{1,0:T(8,128)}), f32[256,256]{1,0:T(8,128)}) %all-reduce.12.cloned.1.call-update) | async-done | bytes 262160 | tf_op jit(solution)/shard_map/psum | solution.py:9
  681.1 1.7 fusion.7
  682.8 1.5 broadcast_select_fusion.1
  684.3 1.0 gather_fusion.7
  685.3 0.9 broadcast_select_fusion
  686.2 0.0 all-reduce.16.cloned.1.call-update
  686.2 0.0 all-reduce.14.cloned.1.call-start
  686.3 210.3 %all-reduce.16.cloned.1.call-done = (f32[256,512]{1,0:T(8,128)}, f32[256,512]{1,0:T(8,128)}) async-done(((f32[256,512]{1,0:T(8,128)}, f32[256,512]{1,0:T(8,128)}), (f32[256,512]{1,0:T(8,128)}, f32[256,512]{1,0:T(8,128)})) %all-reduce.16.cloned.1.call-update) | async-done | bytes 1048592 | tf_op jit(solution)/shard_map/psum | solution.py:9
  896.7 2.3 gather_fusion.6
  899.0 1.0 gather_fusion.8
  900.0 0.1 select_select_fusion
  900.1 1.1 fusion.3
  901.2 0.0 all-reduce.14.cloned.1.call-update
  901.3 114.7 %all-reduce.14.cloned.1.call-done = f32[256,256]{1,0:T(8,128)} async-done(((f32[256,256]{1,0:T(8,128)}), f32[256,256]{1,0:T(8,128)}) %all-reduce.14.cloned.1.call-update) | async-done | bytes 262160 | tf_op jit(solution)/shard_map/psum | solution.py:9
  1016.0 1.7 fusion.8
  1017.7 1.4 fusion
  (43 shorter events, 0.3 us)
Async XLA Ops:
  6.5 0.8 copy-start.8
  6.5 219.4 %all-reduce.20.cloned.1.call-start = ((), (), s32[]{:S(2)}) async-start(), calls=%async_computation.5 | async-start | bytes 2097152 | tf_op jit(solution)/shard_map/psum | solution.py:9
  7.8 2.0 copy-start
  11.7 334.5 %all-reduce.10.cloned.1.call-start = ((), (), s32[]{:S(2)}) async-start(), calls=%async_computation | async-start | bytes 524288 | tf_op jit(solution)/shard_map/psum | solution.py:9
  225.9 2.3 copy-start.1
  229.2 1.1 copy-start.7
  231.5 330.3 %all-reduce.18.cloned.1.call-start = ((), (), s32[]{:S(2)}) async-start(), calls=%async_computation.4 | async-start | bytes 2097152 | tf_op jit(solution)/shard_map/psum | solution.py:9
  346.2 1.7 copy-start.4
  351.3 329.8 %all-reduce.12.cloned.1.call-start = ((), (), s32[]{:S(2)}) async-start(), calls=%async_computation.1 | async-start | bytes 524288 | tf_op jit(solution)/shard_map/psum | solution.py:9
  561.8 2.3 copy-start.2
  566.4 330.3 %all-reduce.16.cloned.1.call-start = ((), (), s32[]{:S(2)}) async-start(), calls=%async_computation.3 | async-start | bytes 2097152 | tf_op jit(solution)/shard_map/psum | solution.py:9
  681.1 1.7 copy-start.5
  686.2 329.8 %all-reduce.14.cloned.1.call-start = ((), (), s32[]{:S(2)}) async-start(), calls=%async_computation.2 | async-start | bytes 524288 | tf_op jit(solution)/shard_map/psum | solution.py:9
  896.7 2.3 copy-start.3
  1016.0 1.7 copy-start.6
Sparse Core Ops, SparseCore 0:
  11.8 214.0 all-reduce.19
  231.6 114.5 all-reduce.9
  351.4 210.2 all-reduce.17
  566.5 114.5 all-reduce.11
  686.3 210.2 all-reduce.15
  901.4 114.5 all-reduce.13
where the time goes:
time: 1030 us
  waiting for transfers between devices  978 us (95%)
  local copies, waits for them, and re-layouts  14.6 us (1%)
  between operations  13.8 us (1%)
  other arithmetic  11.8 us (1%)
    psum x6, waiting for transfers between devices, broadcast(): return lax.psum(jnp.where(mine, array, jnp.zeros_like(array)), axis)  978 us
  transfers between devices with their start and end apart: 6, of which 6 were waited for; matrix products, arithmetic and copies ran while one was open for 0% of the time, Pallas kernels for 0%

commit v1 on v0

--- a/solution.py
+++ b/solution.py
@@ -6,7 +6,7 @@
 
 def broadcast(array, axis, root):
     mine = lax.axis_index(axis) == root
-    return lax.psum(jnp.where(mine, array, jnp.zeros_like(array)), axis)
+    return lax.all_gather(jnp.where(mine, array, jnp.zeros_like(array)), axis).sum(axis=0)
 
 
 def on_device(matrix, pivots, inverses):

time: 1030 us -> 1220 us (1.18)
  the two profiles are of different devices: /device:TPU:2 before, /device:TPU:1 now
where the time goes in v1:
time: 1220 us
  waiting for transfers between devices  1140 us (93%)
  other arithmetic  39.9 us (3%)
  local copies, waits for them, and re-layouts  15 us (1%)
  between operations  13.5 us (1%)
    psum x3, waiting for transfers between devices, on_device(): upper = lax.psum(picked, 'row')  626 us
    all_gather x6, waiting for transfers between devices, broadcast(): lax.all_gather(jnp.where(mine, array, jnp.zeros_like(array)), axis)  513 us
    reduce_sum x6, other arithmetic, broadcast(): lax.all_gather(jnp.where(mine, array, jnp.zeros_like(array)), axis)  30.7 us
  transfers between devices with their start and end apart: 9, of which 9 were waited for; matrix products, arithmetic and copies ran while one was open for 1% of the time, Pallas kernels for 0%

profile of v1, /device:TPU:1, one launch (start us, length us, event | category | flops | bytes accessed | tf_op | source)
XLA Modules:
  0.0 1216.9 jit_solution(3141198002231229392)
XLA Ops:
  6.5 0.8 fusion.45
  7.3 0.8 not_reduce_fusion.2
  8.2 0.3 select_reduce_fusion
  8.5 0.9 compare_select_fusion.1
  9.4 2.3 gather_fusion.1
  11.7 0.9 broadcast_select_fusion.4
  12.7 0.8 broadcast_select_fusion.5
  13.7 0.3 fusion.17
  14.0 212.1 %all-reduce.4.cloned.1.call-done = f32[256,512]{1,0:T(8,128)} async-done(((f32[256,512]{1,0:T(8,128)}), f32[256,512]{1,0:T(8,128)}) %all-reduce.4.cloned.1.call-update) | async-done | bytes 524304 | tf_op jit(solution)/shard_map/psum | solution.py:36
  226.1 2.3 gather_fusion.2
  228.4 106.9 %all-gather.13.cloned.1.call-done = f32[8192,512]{1,0:T(8,128)} async-done(((f32[256,512]{1,0:T(8,128)}), f32[8192,512]{1,0:T(8,128)}) %all-gather.13.cloned.1.call-update) | async-done | bytes 16777232 | tf_op jit(solution)/shard_map/all_gather | solution.py:9
  335.4 7.8 reduce_sum.87
  343.1 1.0 gather_fusion
  344.1 0.1 select_select_fusion.2
  344.3 1.1 fusion.5
  345.4 0.6 compare_reduce_fusion
  346.1 63.7 %all-gather.15.cloned.1.call-done = f32[4096,256]{1,0:T(8,128)} async-done(((f32[256,256]{1,0:T(8,128)}), f32[4096,256]{1,0:T(8,128)}) %all-gather.15.cloned.1.call-update) | async-done | bytes 4194320 | tf_op jit(solution)/shard_map/all_gather | solution.py:9
  409.8 2.5 reduce_sum.90
  412.3 0.7 fusion.6
  413.0 1.5 broadcast_select_fusion.3
  414.4 1.0 gather_fusion.4
  415.4 0.9 broadcast_select_fusion.2
  416.4 0.5 all-gather.17.cloned.1.call-update
  417.1 207.2 %all-reduce.6.cloned.1.call-done = f32[256,512]{1,0:T(8,128)} async-done(((f32[256,512]{1,0:T(8,128)}), f32[256,512]{1,0:T(8,128)}) %all-reduce.6.cloned.1.call-update) | async-done | bytes 524304 | tf_op jit(solution)/shard_map/psum | solution.py:36
  624.3 2.3 gather_fusion.5
  626.6 106.6 %all-gather.17.cloned.1.call-done = f32[8192,512]{1,0:T(8,128)} async-done(((f32[256,512]{1,0:T(8,128)}), f32[8192,512]{1,0:T(8,128)}) %all-gather.17.cloned.1.call-update) | async-done | bytes 16777232 | tf_op jit(solution)/shard_map/all_gather | solution.py:9
  733.2 7.8 reduce_sum.91
  740.9 1.0 gather_fusion.3
  741.9 0.1 select_select_fusion.1
  742.0 1.1 fusion.4
  743.2 0.2 all-reduce.8.cloned.1.call-start
  743.5 64.1 %all-gather.19.cloned.1.call-done = f32[4096,256]{1,0:T(8,128)} async-done(((f32[256,256]{1,0:T(8,128)}), f32[4096,256]{1,0:T(8,128)}) %all-gather.19.cloned.1.call-update) | async-done | bytes 4194320 | tf_op jit(solution)/shard_map/all_gather | solution.py:9
  807.6 2.5 reduce_sum.94
  810.1 0.7 fusion.7
  810.8 1.5 broadcast_select_fusion.1
  812.2 1.0 gather_fusion.7
  813.2 0.9 broadcast_select_fusion
  814.2 0.7 all-gather.21.cloned.1.call-update
  815.0 207.1 %all-reduce.8.cloned.1.call-done = f32[256,512]{1,0:T(8,128)} async-done(((f32[256,512]{1,0:T(8,128)}), f32[256,512]{1,0:T(8,128)}) %all-reduce.8.cloned.1.call-update) | async-done | bytes 524304 | tf_op jit(solution)/shard_map/psum | solution.py:36
  1022.1 2.3 gather_fusion.8
  1024.4 106.9 %all-gather.21.cloned.1.call-done = f32[8192,512]{1,0:T(8,128)} async-done(((f32[256,512]{1,0:T(8,128)}), f32[8192,512]{1,0:T(8,128)}) %all-gather.21.cloned.1.call-update) | async-done | bytes 16777232 | tf_op jit(solution)/shard_map/all_gather | solution.py:9
  1131.3 7.8 reduce_sum.95
  1139.1 1.0 gather_fusion.6
  1140.2 1.1 fusion.3
  1141.4 64.4 %all-gather.23.cloned.1.call-done = f32[4096,256]{1,0:T(8,128)} async-done(((f32[256,256]{1,0:T(8,128)}), f32[4096,256]{1,0:T(8,128)}) %all-gather.23.cloned.1.call-update) | async-done | bytes 4194320 | tf_op jit(solution)/shard_map/all_gather | solution.py:9
  1205.8 2.5 reduce_sum.98
  1208.3 0.7 fusion.8
  1208.9 1.4 fusion
  (51 shorter events, 0.8 us)
Async XLA Ops:
  6.5 219.6 %all-reduce.4.cloned.1.call-start = ((), (), s32[]{:S(2)}) async-start(), calls=%async_computation | async-start | bytes 1048576 | tf_op jit(solution)/shard_map/psum | solution.py:36
  9.4 334.7 %copy-start = (f32[256,512]{1,0:T(8,128)S(1)}, f32[256,512]{1,0:T(8,128)}, u32[]{:S(2)}) copy-start(f32[256,512]{1,0:T(8,128)} %param.9) | copy-start | bytes 1572868
  11.7 332.5 %copy-start.4 = (f32[3,256,256]{2,1,0:T(8,128)S(1)}, f32[3,256,256]{2,1,0:T(8,128)}, u32[]{:S(2)}) copy-start(f32[3,256,256]{2,1,0:T(8,128)} %param.11) | copy-start | bytes 2359300
  12.7 322.7 %all-gather.13.cloned.1.call-start = ((), (), s32[]{:S(2)}) async-start(), calls=%async_computation.3 | async-start | bytes 17301504 | tf_op jit(solution)/shard_map/all_gather | solution.py:9
  13.6 396.2 %all-gather.15.cloned.1.call-start = ((), (), s32[]{:S(2)}) async-start(), calls=%async_computation.4 | async-start | bytes 4456448 | tf_op jit(solution)/shard_map/all_gather | solution.py:9
  226.1 186.9 %copy-start.1 = (f32[256,512]{1,0:T(8,128)S(1)}, f32[256,512]{1,0:T(8,128)}, u32[]{:S(2)}) copy-start(f32[256,512]{1,0:T(8,128)} %all-reduce.4.cloned.1.call-done) | copy-start | bytes 1572868
  345.4 278.9 %all-reduce.6.cloned.1.call-start = ((), (), s32[]{:S(2)}) async-start(), calls=%async_computation.1 | async-start | bytes 1048576 | tf_op jit(solution)/shard_map/psum | solution.py:36
  416.4 316.8 %all-gather.17.cloned.1.call-start = ((), (), s32[]{:S(2)}) async-start(), calls=%async_computation.5 | async-start | bytes 17301504 | tf_op jit(solution)/shard_map/all_gather | solution.py:9
  416.9 390.7 %all-gather.19.cloned.1.call-start = ((), (), s32[]{:S(2)}) async-start(), calls=%async_computation.6 | async-start | bytes 4456448 | tf_op jit(solution)/shard_map/all_gather | solution.py:9
  624.3 186.5 %copy-start.2 = (f32[256,512]{1,0:T(8,128)S(1)}, f32[256,512]{1,0:T(8,128)}, u32[]{:S(2)}) copy-start(f32[256,512]{1,0:T(8,128)} %all-reduce.6.cloned.1.call-done) | copy-start | bytes 1572868
  743.2 278.9 %all-reduce.8.cloned.1.call-start = ((), (), s32[]{:S(2)}) async-start(), calls=%async_computation.2 | async-start | bytes 1048576 | tf_op jit(solution)/shard_map/psum | solution.py:36
  814.1 317.2 %all-gather.21.cloned.1.call-start = ((), (), s32[]{:S(2)}) async-start(), calls=%async_computation.7 | async-start | bytes 17301504 | tf_op jit(solution)/shard_map/all_gather | solution.py:9
  814.9 390.9 %all-gather.23.cloned.1.call-start = ((), (), s32[]{:S(2)}) async-start(), calls=%async_computation.8 | async-start | bytes 4456448 | tf_op jit(solution)/shard_map/all_gather | solution.py:9
  1022.1 186.9 %copy-start.3 = (f32[256,512]{1,0:T(8,128)S(1)}, f32[256,512]{1,0:T(8,128)}, u32[]{:S(2)}) copy-start(f32[256,512]{1,0:T(8,128)} %all-reduce.8.cloned.1.call-done) | copy-start | bytes 1572868
Sparse Core Ops, SparseCore 0:
  12.8 213.2 all-reduce.3
  228.4 106.8 all-gather.12
  345.5 64.2 all-gather.14
  416.5 207.7 all-reduce.5
  626.2 106.8 all-gather.16
  743.3 64.2 all-gather.18
  814.3 207.7 all-reduce.7
  1024.4 106.8 all-gather.20
  1141.4 64.2 all-gather.22
